TPU v7x, 256 devices: a whole 4x4x8 slice. The times are simulated.
256 devices in a mesh: dp: 4 (over y), frame: 64 (over x, z, core).
Axes of the slice: x: 4, y: 4, z: 8, core: 2. Of those that a mesh axis runs over, the one named last changes fastest.
Arguments:
- layer_in: bfloat16 [4, 16384, 2048], P('dp', 'frame'), may hold values from -6 to 6
- in_b: bfloat16 [4, 16384, 128], P('dp', 'frame'), may hold values from -0.5 to 0.5
- in_c: bfloat16 [4, 16384, 128], P('dp', 'frame'), may hold values from -0.5 to 0.5
- dt_raw: float32 [4, 32, 16384], P('dp', None, 'frame'), may hold values from -4 to 4
- a_log: float32 [32], replicated, may hold values from -16 to 1
- skip_gain: float32 [32], replicated, may hold values from 0.5 to 1.5
- dt_bias: float32 [32], replicated, may hold values from -0.5 to 0.5
- foot_map: float32 [12, 2048], replicated, may hold values from -0.125 to 0.125
- contact: int32 [4, 16384], P('dp', 'frame'), may hold values 0 or 1
- out_grad: bfloat16 [4, 16384, 2048], P('dp', 'frame'), may hold values from -27 to 27
Outputs:
- grad_in: bfloat16 [4, 16384, 2048], P('dp', 'frame')
- grad_b: float32 [4, 16384, 128], P('dp', 'frame')
- grad_c: float32 [4, 16384, 128], P('dp', 'frame')
- grad_dt: float32 [4, 32, 16384], P('dp', None, 'frame')
- head_grads: float32 [3, 32], replicated
All inputs are finite; a program needn't handle non-finite values. No bound on the sum of `contact` on one device may be relied on, other than what follows from the above.
Results may differ from a plain program's by a relative error of at most 0.0013.
Values sent between devices are 32-bit elements; how exact they have to be, the bound alone decides.
A program may use at most 320 MiB of HBM per device.

v0:
```python
import jax
import jax.numpy as jnp
from jax import lax
from jax.sharding import PartitionSpec as P

H = 32
P_SIZE = 64
N = 128
GROUP = 128


HIGH = lax.Precision.HIGHEST


def carried_in(array, axis, combine, identity, reverse):
    devices, place = (lax.axis_size(axis), lax.axis_index(axis))
    everything = jax.tree.map(lambda part: lax.all_gather(part, axis), array)
    start = jax.tree.map(
        lambda part, zero: jnp.broadcast_to(jnp.asarray(zero, part.dtype), part.shape),
        array,
        identity,
    )

    def hop(k, before):
        at = devices - 1 - k if reverse else k
        reached = at > place if reverse else at < place
        new = combine(before, jax.tree.map(lambda part: part[at], everything))
        return jax.tree.map(lambda a, b: jnp.where(reached, a, b), new, before)

    return lax.fori_loop(0, devices, hop, start)


def extended(block, sides, width):
    for axis, dim in sides:
        count = lax.axis_size(axis)
        forward = [(i, i + 1) for i in range(count - 1)]
        backward = [(target, source) for source, target in forward]
        low = lax.ppermute(
            lax.slice_in_dim(block, block.shape[dim] - width, None, axis=dim), axis, forward
        )
        high = lax.ppermute(lax.slice_in_dim(block, 0, width, axis=dim), axis, backward)
        block = jnp.concatenate([low, block, high], axis=dim)
    return block


def group_pass(state, pieces, decay_rate, skip_gain):
    block_x, block_b, block_c, block_step = pieces
    width = block_step.shape[1]
    row_ids = lax.broadcasted_iota(jnp.int32, (width, width), 0)
    col_ids = lax.broadcasted_iota(jnp.int32, (width, width), 1)
    upper = (row_ids <= col_ids).astype(jnp.float32)
    logdec = block_step * decay_rate[:, None]
    cumul = jnp.dot(logdec, upper, precision=HIGH)
    causal = (row_ids >= col_ids)[None]
    spread = cumul[:, :, None] - cumul[:, None, :]
    within = jnp.where(causal, jnp.exp(jnp.where(causal, spread, 0.0)), 0.0)
    scores = jnp.dot(block_c, block_b.T, precision=HIGH)
    mixing = scores[None] * within * block_step[:, None, :]
    inner = jnp.einsum("hts,shp->thp", mixing, block_x, precision=HIGH)
    carried = (
        jnp.einsum("tn,hpn->thp", block_c, state, precision=HIGH) * jnp.exp(cumul).T[:, :, None]
    )
    output = inner + carried + skip_gain[None, :, None] * block_x
    tail_weight = jnp.exp(cumul[:, -1:] - cumul) * block_step
    weighted = block_x * tail_weight.T[:, :, None]
    fresh = jnp.einsum("shp,sn->hpn", weighted, block_b, precision=HIGH)
    new_state = jnp.exp(cumul[:, -1])[:, None, None] * state + fresh
    return (new_state, output)


def run_blocks(layer_x, layer_b, layer_c, raw_step, a_log, skip_gain, dt_bias, state):
    length = layer_x.shape[0]
    count = length // GROUP
    step = jax.nn.softplus(raw_step + dt_bias[:, None])
    decay_rate = -jnp.exp(a_log)
    block_x = layer_x.reshape(count, GROUP, H, P_SIZE)
    block_b = layer_b.reshape(count, GROUP, N)
    block_c = layer_c.reshape(count, GROUP, N)
    block_step = step.reshape(H, count, GROUP).transpose(1, 0, 2)

    def advance(carry, pieces):
        return group_pass(carry, pieces, decay_rate, skip_gain)

    final, outputs = lax.scan(
        jax.checkpoint(advance), state, (block_x, block_b, block_c, block_step)
    )
    return (outputs.reshape(length, H * P_SIZE), final)


def combine_states(earlier, later):
    return (earlier[0] * later[0], later[0][:, None, None] * earlier[1] + later[1])


def on_device(layer_in, in_b, in_c, dt_raw, a_log, skip_gain, dt_bias, foot_map, contact, out_grad):
    layer_x = layer_in[0].astype(jnp.float32)
    layer_b = in_b[0].astype(jnp.float32)
    layer_c = in_c[0].astype(jnp.float32)
    raw_step = dt_raw[0]
    given = out_grad[0].astype(jnp.float32)
    touch = contact[0].astype(jnp.float32)[None, :]
    length = layer_x.shape[0]
    step = jax.nn.softplus(raw_step + dt_bias[:, None])
    running = jnp.cumsum(step * (-jnp.exp(a_log))[:, None], axis=1)
    fading = jnp.exp(running)
    total = fading[:, -1]
    empty = jnp.zeros((H, P_SIZE, N), jnp.float32)
    unit = jnp.ones((H,), jnp.float32)
    local_out, local_end = run_blocks(
        layer_x, layer_b, layer_c, raw_step, a_log, skip_gain, dt_bias, empty
    )
    state_in = carried_in((total, local_end), "frame", combine_states, (unit, empty), False)[1]
    carried = jnp.einsum("tn,hpn->thp", layer_c, state_in, precision=HIGH) * fading.T[:, :, None]
    output = local_out + carried.reshape(length, H * P_SIZE)
    velocity = jnp.einsum("kc,tc->kt", foot_map, output, precision=HIGH)
    bundle = jnp.concatenate([velocity, touch], axis=0)
    padded = extended(bundle, (("frame", 1),), 1)
    feet_count = velocity.shape[0]
    before = jnp.concatenate([padded[:feet_count, 0:1], velocity[:, :-1]], axis=1)
    position = lax.broadcasted_iota(jnp.int32, (1, length), 1) + lax.axis_index("frame") * length
    started = (position > 0).astype(jnp.float32)
    slide = touch * started * (velocity - before)
    edge_slide = padded[feet_count:, -1:] * (padded[:feet_count, -1:] - velocity[:, -1:])
    after = jnp.concatenate([slide[:, 1:], edge_slide], axis=1)
    slide_change = slide - after
    cotangent = given + jnp.einsum("kt,kc->tc", slide_change, foot_map, precision=HIGH)
    weighted = cotangent.reshape(length, H, P_SIZE) * fading.T[:, :, None]
    grads_in = carried_in(
        (total, jnp.einsum("thp,tn->hpn", weighted, layer_c, precision=HIGH)),
        "frame",
        combine_states,
        (unit, empty),
        True,
    )[1]

    def forward(part_x, part_b, part_c, part_step, part_log, part_skip, part_bias):
        return run_blocks(
            part_x, part_b, part_c, part_step, part_log, part_skip, part_bias, state_in
        )

    _, pull = jax.vjp(forward, layer_x, layer_b, layer_c, raw_step, a_log, skip_gain, dt_bias)
    grad_x, grad_b, grad_c, grad_step, grad_log, grad_skip, grad_bias = pull((cotangent, grads_in))
    head_grads = lax.psum(jnp.stack([grad_log, grad_skip, grad_bias]), ("dp", "frame"))
    return (
        grad_x.astype(jnp.bfloat16)[None],
        grad_b[None],
        grad_c[None],
        grad_step[None],
        head_grads,
    )


def solution(mesh):
    return jax.shard_map(
        on_device,
        mesh=mesh,
        in_specs=(
            P("dp", "frame", None),
            P("dp", "frame", None),
            P("dp", "frame", None),
            P("dp", None, "frame"),
            P(),
            P(),
            P(),
            P(),
            P("dp", "frame"),
            P("dp", "frame", None),
        ),
        out_specs=(
            P("dp", "frame", None),
            P("dp", "frame", None),
            P("dp", "frame", None),
            P("dp", None, "frame"),
            P(),
        ),
        check_vma=False,
    )
```

profile of v0, /device:TPU:1, one launch (start us, length us, event | category | flops | bytes accessed | tf_op | source)
XLA Modules:
  0.0 1031.4 jit_solution(862115234054087157)
XLA Ops:
  9.9 4.5 reshape.248
  14.4 3.8 copy.143
  20.6 78.1 %while.84 = (s32[]{:T(128)}, f32[32,64,128]{2,1,0:T(8,128)S(1)}, f32[2,128,32,64]{1,0,3,2:T(2,128)}, f32[2,32,128]{2,1,0:T(8,128)}, f32[32]{0:T(128)}, /*index=5...) while((s32[]{:T(128)}, f32[32,64,128]{2,1,0:T(8,128)S(1)}, ...), condition=%wide.region_3.4_spmd.clone, body=%wide.region_2.3_spmd.clone.sunk | while | flops 1244442624 | bytes 12178852 | solution.py:84
  22.5 5.3 fusion.234
  29.3 3.2 fusion.235
  32.5 24.9 %dynamic_update_slice.64 = f32[2,128,32,64]{1,0,3,2:T(2,128)} dynamic-update-slice(f32[2,128,32,64]{1,0,3,2:T(2,128)} %get-tuple-element.1480, f32[1,128,32,64]{1,0,3,2:T(1,128)} %bitcast.349, s32[]{:T(128)} %get-tuple-element.1478, s32[]{:T(128)} %constant.170.clone.1..sunk, s32[]{:T(128)} %constant.170.clone.1..sunk, s32[]{:T(128)} %constant.170.clone.1..sunk) | dynamic-update-slice | bytes 2097156 | tf_op jit(solution)/shard_map/while/body/jit(dynamic_update_index_in_dim)/dynamic_update_slice | solution.py:84
  61.5 5.3 fusion.234
  68.3 3.2 fusion.235
  71.5 24.9 %dynamic_update_slice.64 = f32[2,128,32,64]{1,0,3,2:T(2,128)} dynamic-update-slice(f32[2,128,32,64]{1,0,3,2:T(2,128)} %get-tuple-element.1480, f32[1,128,32,64]{1,0,3,2:T(1,128)} %bitcast.349, s32[]{:T(128)} %get-tuple-element.1478, s32[]{:T(128)} %constant.170.clone.1..sunk, s32[]{:T(128)} %constant.170.clone.1..sunk, s32[]{:T(128)} %constant.170.clone.1..sunk) | dynamic-update-slice | bytes 2097156 | tf_op jit(solution)/shard_map/while/body/jit(dynamic_update_index_in_dim)/dynamic_update_slice | solution.py:84
  104.3 133.4 %all-reduce.2 = f32[2048]{0:T(1024)S(1)} all-reduce(f32[2048]{0:T(1024)S(1)} %dynamic-update-slice), channel_id=2, replica_groups=mesh['dp'=4,'frame'=64] {'frame'}, use_global_device_ids=true, to_apply=%add.2 | all-reduce | flops 2048 | bytes 16384
  240.0 3.0 copy.145
  242.9 98.5 %all-gather.6.cloned.1.call-done = f32[2048,64,128]{2,1,0:T(8,128)} async-done(((f32[32,64,128]{2,1,0:T(8,128)}), f32[2048,64,128]{2,1,0:T(8,128)}) %all-gather.6.cloned.1.call-update) | async-done | bytes 67108880 | tf_op jit(solution)/shard_map/all_gather | solution.py:17
  341.5 96.2 %while.85 = (s32[]{:T(128)}, f32[32,64,128]{2,1,0:T(8,128)S(1)}, s32[]{:T(128)}, f32[64,32]{1,0:T(8,128)S(1)}, f32[64,32,64,128]{3,2,1,0:T(8,128)}, /*index=5*/s32[]{:T(128)}, s32[]{:T(128)}) while((s32[]{:T(128)}, f32[32,64,128]{2,1,0:T(8,128)S(1)}, s32[]{:T(128)}, f32[64,32]{1,0:T(8,128)S(1)}, f32[64,32,64,128]{3,2,1,0:T(8,128)}, ...), condition=%wide.region_5.6_spmd.clone, body=%wide.region_4.5_spmd.clone.sunk | while | flops 1048580 | bytes 3146217 | solution.py:30
  448.7 4.1 fusion.152
  452.8 2.9 copy.146
  455.7 3.6 fusion.133
  459.4 9.5 while.83
  468.9 4.9 reshape.246
  473.8 5.0 copy.151
  478.8 217.3 %all-gather.8.cloned.1.call-done = f32[2048,64,128]{2,1,0:T(8,128)} async-done(((f32[32,64,128]{2,1,0:T(8,128)}), f32[2048,64,128]{2,1,0:T(8,128)}) %all-gather.8.cloned.1.call-update) | async-done | bytes 67108880 | tf_op jit(solution)/shard_map/all_gather | solution.py:17
  696.2 139.5 %while.86 = (s32[]{:T(128)}, f32[32,64,128]{2,1,0:T(8,128)S(1)}, s32[]{:T(128)}, f32[64,32]{1,0:T(8,128)}, f32[64,32,64,128]{3,2,1,0:T(8,128)}, /*index=5*/s32[]{:T(128)}, s32[]{:T(128)}, s32[]{:T(128)}, s32[]{:T(128)}) while((s32[]{:T(128)}, f32[32,64,128]{2,1,0:T(8,128)S(1)}, s32[]{:T(128)}, f32[64,32]{1,0:T(8,128)}, ...), condition=%wide.region_7.8_spmd.clone, body=%wide.region_6.7_spmd.clone.sunk | while | flops 1048584 | bytes 3146279 | solution.py:30
  838.8 100.8 %while.87 = (s32[]{:T(128)}, f32[32]{0:T(128)}, f32[32]{0:T(128)}, f32[32,64,128]{2,1,0:T(8,128)S(1)}, bf16[2,128,32,64]{1,3,2,0:T(8,128)(2,1)}, /*index=5*/f32[...) while((s32[]{:T(128)}, f32[32]{0:T(128)}, f32[32]{0:T(128)}, ...), condition=%wide.region_21.22_spmd.clone, body=%wide.region_10.21_spmd.clone.sunk | while | flops 2921738240 | bytes 57451836 | solution.py:84
  850.2 2.9 dynamic-slice_bitcast_fusion.18
  854.1 3.9 multiply_reduce_fusion.10
  866.5 6.7 fusion.259
  885.8 3.1 convolution_bitcast_fusion.4
  894.8 2.9 dynamic-slice_bitcast_fusion.18
  898.7 3.9 multiply_reduce_fusion.10
  911.1 6.7 fusion.259
  930.4 3.1 convolution_bitcast_fusion.4
  942.9 74.3 %psum.7 = f32[3,32]{1,0:T(4,128)} all-reduce(f32[3,32]{1,0:T(4,128)S(1)} %pad_maximum_fusion.1), channel_id=1, replica_groups=mesh['dp'=4,'frame'=64] {'dp','frame'}, use_global_device_ids=true, to_apply=%region_23.24 | all-reduce | flops 96 | bytes 768 | tf_op jit(solution)/shard_map/psum | solution.py:142
  1017.2 3.9 copy.159
  (557 shorter events, 340.7 us)
Async XLA Ops:
  7.2 431.5 %copy-start = (f32[12,2048]{1,0:T(8,128)S(1)}, f32[12,2048]{1,0:T(8,128)}, u32[]{:S(2)}) copy-start(f32[12,2048]{1,0:T(8,128)} %param.27) | copy-start | bytes 294916
  7.2 334.3 %all-gather.6.cloned.1.call-start = ((), (), s32[]{:S(2)}) async-start(), calls=%async_computation | async-start | bytes 68157440 | tf_op jit(solution)/shard_map/all_gather | solution.py:17
  14.4 3.8 copy-start.34
  14.4 4.7 copy-start.44
  99.6 596.5 %all-gather.8.cloned.1.call-start = ((), (), s32[]{:S(2)}) async-start(), calls=%async_computation.1 | async-start | bytes 68157440 | tf_op jit(solution)/shard_map/all_gather | solution.py:17
  341.5 96.2 %copy-start.23 = (bf16[1,256,128]{2,1,0:T(8,128)(2,1)S(1)}, bf16[1,256,128]{2,1,0:T(8,128)(2,1)}, u32[]{:S(2)}) copy-start(bf16[1,256,128]{2,1,0:T(8,128)(2,1)} %param.22) | copy-start | bytes 196612
  439.3 9.4 copy-start.10
  439.3 9.4 copy-start.22
  440.5 4.3 collective-permute-start
  442.5 5.0 collective-permute-start.1
  866.4 6.8 copy-start.24
  866.5 6.7 copy-start.26
  878.4 6.7 copy-start.11
  884.1 5.8 copy-start.4
  885.7 4.2 copy-start.14
  885.7 4.2 copy-start.17
  885.7 4.2 copy-start.18
  885.8 4.2 copy-start.20
  885.8 4.2 copy-start.25
  885.8 4.2 copy-start.27
  885.8 4.2 copy-start.43
  911.1 6.8 copy-start.24
  911.1 6.7 copy-start.26
  923.0 6.7 copy-start.11
  928.8 5.8 copy-start.4
  930.4 4.2 copy-start.14
  930.4 4.2 copy-start.17
  930.4 4.2 copy-start.18
  930.4 4.2 copy-start.20
  930.4 4.2 copy-start.25
  930.4 4.2 copy-start.27
  930.4 4.2 copy-start.43
  (53 other events, 109.1 us)
Sparse Core Ops, SparseCore 0:
  99.8 241.6 all-gather.5
  459.4 236.6 all-gather.7
where the time goes:
time: 1050 us; the launch traced here: 1030 us
  waiting for transfers between devices  318 us (30%)
  other arithmetic  212 us (20%)
  blocking collectives  208 us (20%)
  local copies, waits for them, and re-layouts  170 us (16%)
  matrix products  88 us (8%)
  loops' own time  16.1 us (2%)
  between operations  15.2 us (1%)
    all_gather x2, waiting for transfers between devices, carried_in(): everything = jax.tree.map(lambda part: lax.all_gather(part, axis), array)  316 us
    select_n x128, other arithmetic, hop(): return jax.tree.map(lambda a, b: jnp.where(reached, a, b), new, before)  187 us
    unnamed x1, blocking collectives  133 us
    psum x1, blocking collectives, on_device(): lax.psum(jnp.stack([grad_log, grad_skip, grad_bias]), ('dp', 'frame'))  74.3 us
    dynamic_update_slice x4, local copies, waits for them, and re-layouts, run_blocks(): lax.scan(jax.checkpoint(advance), state, (block_x, block_b, block_c, bloc...  52 us
    mul x128, local copies, waits for them, and re-layouts, combine_states(): later[0][:, None, None] * earlier[1] + later[1]  45.2 us
    dot_general x6, matrix products, group_pass(): inner = jnp.einsum('hts,shp->thp', mixing, block_x, precision=HIGH)  29.1 us
  transfers between devices with their start and end apart: 4, of which 3 were waited for; matrix products, arithmetic and copies ran while one was open for 3% of the time, Pallas kernels for 0%

commit v1 on v0

v1 whole, which is shorter than its diff:
```python
import functools

import jax
import jax.numpy as jnp
from jax import lax
from jax.experimental import pallas as pl
from jax.experimental.pallas import tpu as pltpu
from jax.sharding import PartitionSpec as P

MESH = pl.DeviceIdType.MESH
HIGH = lax.Precision.HIGHEST
F32, BF16 = jnp.float32, jnp.bfloat16
H, PS, N, T, HP, FEET = 32, 64, 128, 256, 2048, 12
PAIRS = HP // 128
LOG2E = 1.4426950408889634
KL = 512
G1 = 16


def nn(a, b):
    return lax.dot_general(a, b, (((1,), (0,)), ((), ())), preferred_element_type=F32)


def nt(a, b):
    return lax.dot_general(a, b, (((1,), (1,)), ((), ())), preferred_element_type=F32)


def nn_hi(a, b):
    return lax.dot_general(
        a, b, (((1,), (0,)), ((), ())), precision=HIGH, preferred_element_type=F32
    )


def nt_hi(a, b):
    return lax.dot_general(
        a, b, (((1,), (1,)), ((), ())), precision=HIGH, preferred_element_type=F32
    )


def split(v):
    hi = v.astype(BF16)
    return hi, (v - hi.astype(F32)).astype(BF16)


def split3(v):
    hi = v.astype(BF16)
    rest = v - hi.astype(F32)
    mid = rest.astype(BF16)
    return hi, mid, (rest - mid.astype(F32)).astype(BF16)


def iota(shape, dim):
    return lax.broadcasted_iota(jnp.int32, shape, dim)


def kernel(
    dp_n,
    nf,
    x_ref,
    b_ref,
    c_ref,
    dt_ref,
    al_ref,
    sk_ref,
    bi_ref,
    f_ref,
    ct_ref,
    og_ref,
    gx_ref,
    gb_ref,
    gc_ref,
    gdt_ref,
    hg_ref,
    local_f,
    local_r,
    sib_f,
    sib_r,
    half_f,
    half_r,
    got_f,
    got_r,
    ret_f,
    ret_r,
    s_in,
    g_end,
    cexp,
    sexp,
    yv,
    dz,
    zhi,
    zlo,
    dyhi,
    dylo,
    fpad,
    c2_ref,
    ld_ref,
    sg_ref,
    sc_ref,
    sct_ref,
    ds0,
    ds1,
    dec_mine,
    decs,
    sib_dec,
    dec_all,
    vel,
    vel_prev,
    vel_next,
    gd_local,
    gd_got,
    gd_ret,
    gd_end,
    p1,
    p2,
    row_d,
    row_b,
    hsum,
    hgot1,
    hmid,
    hgot2,
    ssem,
    rsem,
):
    chips = nf // 2
    me_dp = lax.axis_index("dp")
    me = lax.axis_index("frame")
    chip, core = me // 2, me % 2
    sib = me + 1 - 2 * core
    first = core == 0
    lbs = chips // 8
    lanes = HP // lbs
    g2n = dp_n * (nf // G1)

    def ring(k, base=None):
        return lax.rem(me + k, nf)

    barrier = pltpu.get_barrier_semaphore()

    @pl.loop(1, nf)
    def _(k):
        pl.semaphore_signal(barrier, inc=1, device_id=(me_dp, ring(k)), device_id_type=MESH)

    group = me // G1
    low = me % G1

    @pl.loop(1, dp_n)
    def _(k):
        d = lax.rem(me_dp + k, dp_n)

        @pl.loop(0, nf // G1)
        def _(j):
            pl.semaphore_signal(
                barrier, inc=1, device_id=(d, j * G1 + low), device_id_type=MESH
            )

    def remote(src, dst, s, r, dev, dp=None):
        return pltpu.make_async_remote_copy(
            src_ref=src,
            dst_ref=dst,
            send_sem=ssem.at[s],
            recv_sem=rsem.at[r],
            device_id=(me_dp if dp is None else dp, dev),
            device_id_type=MESH,
        )

    eye = (iota((T, T), 0) == iota((T, T), 1)).astype(F32)
    rows8 = iota((8, H), 0)
    rows = jnp.where(
        rows8 == 0, al_ref[...], jnp.where(rows8 == 1, sk_ref[...], bi_ref[...])
    )
    eye32 = (iota((H, H), 0) == iota((H, H), 1)).astype(F32)
    cols = nt_hi(eye32, rows)
    rate = -jnp.exp(cols[:, 0:1])
    raw = dt_ref[...] + cols[:, 2:3]
    tail = jnp.exp(-jnp.abs(raw))
    step = jnp.maximum(raw, 0.0) + jnp.log1p(tail)
    sg_ref[...] = jnp.where(raw >= 0, 1.0, tail) / (1.0 + tail)
    ld = rate * step
    ld_ref[...] = ld
    upper = (iota((T, T), 0) <= iota((T, T), 1)).astype(F32)
    c2 = nn_hi(ld, upper) * LOG2E
    for i in range(PAIRS):
        c2_ref[i, 0:2, :] = c2[2 * i : 2 * i + 2]
    c3 = jnp.concatenate(split3(nt_hi(eye, c2)), axis=1)
    s3 = jnp.concatenate(split3(nt_hi(eye, step)), axis=1)
    spread_k = (iota((96, KL), 0) % H == iota((96, KL), 1) % H).astype(BF16)
    c_feet = nn(c3, spread_k)
    dec_mine[...] = jnp.broadcast_to(c_feet[T - 1 : T, 0:128], (8, 128))
    eye_b = (iota((N, N), 0) == iota((N, N), 1)).astype(BF16)
    bb, cc = b_ref[...], c_ref[...]
    bt = nt(eye_b, bb).astype(BF16)
    ct = nt(eye_b, cc).astype(BF16)

    fpad[...] = jnp.zeros_like(fpad)
    fpad[0:FEET, :] = f_ref[...]

    @pl.loop(0, PAIRS)
    def _(i):
        blk = pl.ds(pl.multiple_of(i * 128, 128), 128)
        e3 = (iota((96, 128), 0) % H == 2 * i + iota((96, 128), 1) // PS).astype(BF16)
        cb, sb = nn(c3, e3), nn(s3, e3)
        cexp[:, blk] = cb
        sexp[:, blk] = sb
        z = sb * x_ref[:, blk].astype(F32)
        hi, lo = split(z)
        zhi[:, blk] = hi
        zlo[:, blk] = lo
        hi, lo = split(jnp.exp2(cb[T - 1 : T] - cb) * z)
        local_f[:, blk] = nn(bt, hi) + nn(bt, lo)
        hi, lo = split(jnp.exp2(cb) * og_ref[:, blk].astype(F32))
        local_r[:, blk] = nn(ct, hi) + nn(ct, lo)

    pl.semaphore_wait(barrier, nf - 1 + (dp_n - 1) * (nf // G1))

    mine_half = pl.ds(pl.multiple_of(core * 64, 64), 64)
    sib_half = pl.ds(pl.multiple_of(64 - core * 64, 64), 64)
    ex_dec = remote(dec_mine, sib_dec, 5, 5, sib)
    ex = [
        remote(local_f.at[sib_half], sib_f.at[sib_half], 1, 1, sib),
        remote(local_r.at[sib_half], sib_r.at[sib_half], 2, 2, sib),
        remote(local_f.at[mine_half], sib_f.at[mine_half], 3, 3, sib),
        remote(local_r.at[mine_half], sib_r.at[mine_half], 4, 4, sib),
    ]
    ex_dec.start()
    ex[0].start()
    ex[1].start()

    @pl.loop(1, nf)
    def _(k):
        remote(dec_mine, decs.at[me], 0, 0, ring(k)).start()

    decs[me] = dec_mine[...]

    scores = nt(cc, bb)
    sc_ref[...] = jnp.where(iota((T, T), 0) >= iota((T, T), 1), scores, 0.0)
    scores = nt(bb, cc)
    sct_ref[...] = jnp.where(iota((T, T), 0) <= iota((T, T), 1), scores, 0.0)

    def sib_decay(i):
        e1 = (iota((128, 128), 0) == 2 * i + iota((128, 128), 1) // PS).astype(F32)
        return jnp.exp2(nn_hi(sib_dec[...], e1))[0:1]

    ex_dec.wait()
    ex[0].wait()
    ex[1].wait()

    @pl.loop(0, PAIRS)
    def _(i):
        blk = pl.ds(pl.multiple_of(i * 128, 128), 128)
        d_sib = sib_decay(i)
        d_me = jnp.exp2(cexp[pl.ds(T - 8, 8), blk])[7:8]
        one = jnp.ones_like(d_me)
        half_f[:, blk] = (
            jnp.where(first, d_sib, one) * local_f[mine_half, blk]
            + jnp.where(first, one, d_me) * sib_f[mine_half, blk]
        )
        half_r[:, blk] = (
            jnp.where(first, one, d_sib) * local_r[mine_half, blk]
            + jnp.where(first, d_me, one) * sib_r[mine_half, blk]
        )

    def part(o):
        return (
            pl.ds(pl.multiple_of(o // lbs * 8, 8), 8),
            pl.ds(pl.multiple_of(o % lbs * lanes, 128), lanes),
        )

    @pl.loop(1, chips)
    def _(k):
        o = lax.rem(chip + k, chips)
        r, l = part(o)
        remote(half_f.at[r, l], got_f.at[chip], 6, 6, o * 2 + core).start()
        remote(half_r.at[r, l], got_r.at[chip], 7, 7, o * 2 + core).start()

    ex[2].start()
    ex[3].start()
    my_r, my_l = part(chip)
    got_f[chip] = half_f[my_r, my_l]
    got_r[chip] = half_r[my_r, my_l]

    low_lanes = iota((128, 128), 1) < PS

    def inner(i):
        blk = pl.ds(pl.multiple_of(i * 128, 128), 128)
        rhs = jnp.concatenate([zhi[:, blk], zlo[:, blk]], axis=1)
        cb = cexp[:, blk]
        for r in range(2):
            seen = 128 * (r + 1)
            at = slice(128 * r, seen)
            outs = []
            for e in range(2):
                col = cb[at, PS * e : PS * e + 1]
                row = c2_ref[i, e : e + 1, 0:seen]
                mix = sc_ref[at, 0:seen] * jnp.exp2(jnp.minimum(col - row, 0.0))
                hi, lo = split(mix)
                res = nn(hi, rhs[0:seen]) + nn(lo, rhs[0:seen])
                outs.append(res[:, 0:128] + res[:, 128:256])
            yv[at, blk] = jnp.where(low_lanes, outs[0], outs[1])

    pl.loop(0, PAIRS // 2)(inner)

    def arrived(buf, n, s):
        view = buf.at[pl.ds(0, n)]
        d = remote(view, view, s, s, sib)
        d.wait()

    arrived(decs, nf - 1, 0)
    dall = decs[:, 0, :]
    dec_all[...] = jnp.exp2(dall)
    pairsum = (iota((chips, nf), 0) == iota((chips, nf), 1) // 2).astype(F32)
    chip_log = nn_hi(pairsum, dall)
    head0 = chip % lbs * (lanes // PS)
    spread_l = (iota((128, lanes), 0) == head0 + iota((128, lanes), 1) // PS).astype(F32)
    chip_dec = jnp.exp2(nn_hi(chip_log, spread_l))

    arrived(got_f, chips - 1, 6)
    acc = jnp.zeros((8, lanes), F32)
    for q in range(chips):
        ret_f[q] = acc
        acc = got_f[q] + chip_dec[q : q + 1] * acc

    @pl.loop(1, chips)
    def _(k):
        o = lax.rem(chip + k, chips)
        r = pl.ds(pl.multiple_of(core * 64 + chip // lbs * 8, 8), 8)
        remote(ret_f.at[o], s_in.at[r, my_l], 8, 8, o * 2 + core).start()

    arrived(got_r, chips - 1, 7)
    acc = jnp.zeros((8, lanes), F32)
    for q in reversed(range(chips)):
        ret_r[q] = acc
        acc = got_r[q] + chip_dec[q : q + 1] * acc

    @pl.loop(1, chips)
    def _(k):
        o = lax.rem(chip + k, chips)
        r = pl.ds(pl.multiple_of(core * 64 + chip // lbs * 8, 8), 8)
        remote(ret_r.at[o], g_end.at[r, my_l], 9, 9, o * 2 + core).start()

    own = pl.ds(pl.multiple_of(core * 64 + chip // lbs * 8, 8), 8)
    s_in[own, my_l] = ret_f[chip]
    g_end[own, my_l] = ret_r[chip]

    pl.loop(PAIRS // 2, PAIRS)(inner)

    arrived(ret_f, chips - 1, 8)
    back_f = remote(s_in.at[mine_half], s_in.at[mine_half], 10, 10, sib)
    back_f.start()
    ex[2].wait()
    ex[3].wait()
    back_f.wait()

    vel[...] = jnp.zeros_like(vel)
    sk8 = jnp.broadcast_to(sk_ref[...], (8, H))

    @pl.loop(0, PAIRS)
    def _(i):
        blk = pl.ds(pl.multiple_of(i * 128, 128), 128)
        d_sib = sib_decay(i)
        state = s_in[:, blk]
        state = jnp.where(first, state, sib_f[:, blk] + d_sib * state)
        s_in[:, blk] = state
        hi, lo = split(state)
        y = yv[:, blk] + jnp.exp2(cexp[:, blk]) * (nn(cc, hi) + nn(cc, lo))
        yv[:, blk] = y
        e1 = (iota((H, 128), 0) == 2 * i + iota((H, 128), 1) // PS).astype(F32)
        out = y + nn_hi(sk8, e1)[0:1] * x_ref[:, blk].astype(F32)
        hi, lo = split(out)
        fhi, flo = split(fpad[:, blk])
        vel[...] += nt(hi, fhi) + nt(lo, fhi) + nt(hi, flo)

    touch = jnp.broadcast_to(ct_ref[...].astype(F32), (8, T))
    touch = nt_hi(eye, touch)[:, 0:1]
    lane = iota((T, 128), 1)
    row = iota((T, 128), 0)
    v = jnp.where(lane == FEET, touch, vel[...])
    vel[...] = v
    to_next = remote(vel.at[pl.ds(T - 8, 8)], vel_prev, 12, 12, ring(1))
    to_prev = remote(vel.at[pl.ds(0, 8)], vel_next, 13, 13, ring(nf - 1))
    to_next.start()
    to_prev.start()
    to_next.wait()
    to_prev.wait()
    feet = lane < FEET
    before = jnp.where(row == 0, vel_prev[7:8, :], pltpu.roll(v, 1, 0))
    slide = jnp.where(
        feet & ((row > 0) | (me > 0)), touch * (v - before), 0.0
    )
    nxt = vel_next[0:1, :]
    edge = nxt[:, FEET : FEET + 1] * (nxt - v[T - 1 : T, :])
    edge = jnp.where((iota((1, 128), 1) < FEET) & (me < nf - 1), edge, 0.0)
    change = slide - jnp.where(row == T - 1, edge, pltpu.roll(slide, T - 1, 0))
    chi, clo = split(change)

    feet_of = (iota((128, KL), 0) == iota((128, KL), 1) // H).astype(BF16)
    hi, lo = split(jnp.exp2(c_feet) * (nn(chi, feet_of) + nn(clo, feet_of)))
    gd_local[...] = nn(ct, hi) + nn(ct, lo)

    def tile(o):
        return (
            pl.ds(pl.multiple_of(o // 4 * 8, 8), 8),
            pl.ds(pl.multiple_of(o % 4 * 128, 128), 128),
        )

    @pl.loop(1, nf)
    def _(k):
        o = ring(k)
        r, l = tile(o)
        remote(gd_local.at[r, l], gd_got.at[me], 14, 14, o).start()

    my_tr, my_tl = tile(me)
    gd_got[me] = gd_local[my_tr, my_tl]

    arrived(ret_r, chips - 1, 9)
    back_r = remote(g_end.at[mine_half], g_end.at[mine_half], 11, 11, sib)
    back_r.start()

    @pl.loop(0, PAIRS)
    def _(i):
        blk = pl.ds(pl.multiple_of(i * 128, 128), 128)
        fhi, flo = split(fpad[:, blk])
        dy = og_ref[:, blk].astype(F32) + nn(chi, fhi) + nn(clo, fhi) + nn(chi, flo)
        hi, lo = split(dy)
        dyhi[:, blk] = hi
        dylo[:, blk] = lo

    ds0[...] = jnp.zeros_like(ds0)
    ds1[...] = jnp.zeros_like(ds1)
    zero_b = jnp.zeros((128, 128), BF16)

    def backward(i):
        blk = pl.ds(pl.multiple_of(i * 128, 128), 128)
        dh, dl = dyhi[:, blk], dylo[:, blk]
        rhs = jnp.concatenate([dh, dl], axis=1)
        twice = jnp.concatenate([dh, dh], axis=1)
        cb = cexp[:, blk]
        for r, acc in ((0, ds0), (1, ds1)):
            at, on = slice(128 * r, 128 * r + 128), slice(128 * r, T)
            zh, zl = zhi[at, blk], zlo[at, blk]
            outs = []
            total = acc[...]
            for e in range(2):
                keep = low_lanes if e == 0 else ~low_lanes
                zhe = jnp.where(keep, zh, zero_b)
                zle = jnp.where(keep, zl, zero_b)
                col = cb[at, PS * e : PS * e + 1]
                fall = jnp.exp2(jnp.minimum(c2_ref[i, e : e + 1, on] - col, 0.0))
                w = nt(jnp.concatenate([zhe, zle], axis=1), twice[on]) + nt(zhe, dl[on])
                total = total + fall * w
                hi, lo = split(sct_ref[at, on] * fall)
                res = nn(hi, rhs[on]) + nn(lo, rhs[on])
                outs.append(res[:, 0:128] + res[:, 128:256])
            acc[...] = total
            dz[at, blk] = jnp.where(low_lanes, outs[0], outs[1])

    pl.loop(0, PAIRS // 2)(backward)

    arrived(gd_got, nf - 1, 14)
    acc = jnp.zeros((8, 128), F32)
    for q in reversed(range(nf)):
        gd_ret[q] = acc
        acc = gd_got[q] + dec_all[q : q + 1] * acc

    @pl.loop(1, nf)
    def _(k):
        o = ring(k)
        remote(gd_ret.at[o], gd_end.at[my_tr, my_tl], 15, 15, o).start()

    gd_end[my_tr, my_tl] = gd_ret[me]

    pl.loop(PAIRS // 2, PAIRS)(backward)

    m0 = iota((128, T), 0) <= iota((128, T), 1)
    m1 = iota((128, 128), 0) <= iota((128, 128), 1)
    dst = jnp.concatenate(
        [
            jnp.where(m0, ds0[...], 0.0),
            jnp.concatenate(
                [jnp.zeros((128, 128), F32), jnp.where(m1, ds1[...], 0.0)], axis=1
            ),
        ],
        axis=0,
    )
    hi, lo = split(dst)
    gb_ref[...] = nn(hi, cc) + nn(lo, cc)
    eye_t = eye.astype(BF16)
    hi = nt(eye_t, hi).astype(BF16)
    lo = nt(eye_t, lo).astype(BF16)
    gc_ref[...] = nn(hi, bb) + nn(lo, bb)

    @pl.loop(0, PAIRS)
    def _(i):
        blk = pl.ds(pl.multiple_of(i * 128, 128), 128)
        dy = dyhi[:, blk].astype(F32) + dylo[:, blk].astype(F32)
        hi, lo = split(jnp.exp2(cexp[:, blk]) * dy)
        shi, slo = split(s_in[:, blk])
        gc_ref[...] += nt(hi, shi) + nt(lo, shi) + nt(hi, slo)

    back_r.wait()
    view = gd_ret.at[pl.ds(0, nf - 1)]
    remote(view, view, 15, 15, sib).wait()

    p1[...] = jnp.zeros_like(p1)
    p2[...] = jnp.zeros_like(p2)
    gdh, gdl = split(gd_end[:, 0 : FEET * H])

    @pl.loop(0, PAIRS)
    def _(i):
        blk = pl.ds(pl.multiple_of(i * 128, 128), 128)
        here = iota((H, 128), 0) == 2 * i + iota((H, 128), 1) // PS
        e1 = here.astype(F32)
        e1b = here.astype(BF16)
        ff = fpad[0:16, blk]
        big = jnp.concatenate([ff[k : k + 1] * e1 for k in range(FEET)], axis=0)
        bhi, blo = split(big)
        grad = g_end[:, blk]
        grad = jnp.where(first, sib_r[:, blk] + sib_decay(i) * grad, grad)
        grad = grad + nn(gdh, bhi) + nn(gdl, bhi) + nn(gdh, blo)
        ghi, glo = split(grad)
        cb, sb = cexp[:, blk], sexp[:, blk]
        last = cb[T - 1 : T]
        fade = jnp.exp2(last - cb)
        x = x_ref[:, blk].astype(F32)
        dzb = dz[:, blk] + fade * (nn(bb, ghi) + nn(bb, glo))
        dy = dyhi[:, blk].astype(F32) + dylo[:, blk].astype(F32)
        gx_ref[:, blk] = (nn_hi(sk8, e1)[0:1] * dy + sb * dzb).astype(BF16)
        xdz = x * dzb
        hi, lo = split(xdz)
        p2[...] += nt(e1b, hi) + nt(e1b, lo)
        hi, lo = split(yv[:, blk] * dy - sb * xdz)
        p1[...] += nt(e1b, hi) + nt(e1b, lo)
        hi, lo = split(fade * sb * x)
        gb_ref[...] += nt(hi, ghi) + nt(lo, ghi) + nt(hi, glo)
        s_last = jnp.exp2(last) * s_in[:, blk] + local_f[:, blk]
        row_d[:, blk] = jnp.broadcast_to(jnp.sum(x * dy, axis=0, keepdims=True), (8, 128))
        row_b[:, blk] = jnp.broadcast_to(jnp.sum(grad * s_last, axis=0, keepdims=True), (8, 128))

    heads = (iota((H, HP), 0) == iota((H, HP), 1) // PS).astype(F32)
    edge_h = nt_hi(heads, row_b[...])[:, 0:1]
    skip_h = nt_hi(row_d[...], heads)
    later = (iota((T, T), 0) >= iota((T, T), 1)).astype(F32)
    dld = nn_hi(p1[...], later) + edge_h
    gdt = (rate * dld + p2[...]) * sg_ref[...]
    gdt_ref[...] = gdt
    ones8 = jnp.ones((8, T), F32)
    log_h = nt_hi(ones8, dld * ld_ref[...])
    bias_h = nt_hi(ones8, gdt)
    hsum[...] = jnp.zeros_like(hsum)
    hsum[:, 0:H] = jnp.where(rows8 == 0, log_h, jnp.where(rows8 == 1, skip_h, bias_h))

    @pl.loop(1, G1)
    def _(k):
        j = lax.rem(low + k, G1)
        remote(hsum, hgot1.at[low], 16, 16, group * G1 + j).start()

    hgot1[low] = hsum[...]
    arrived(hgot1, G1 - 1, 16)
    hmid[...] = jnp.sum(hgot1[...], axis=0)
    spot = me_dp * (nf // G1) + group

    @pl.loop(1, g2n)
    def _(k):
        j = lax.rem(spot + k, g2n)
        remote(
            hmid, hgot2.at[spot], 17, 17, j % (nf // G1) * G1 + low, j // (nf // G1)
        ).start()

    hgot2[spot] = hmid[...]
    arrived(hgot2, g2n - 1, 17)
    hg_ref[...] = jnp.sum(hgot2[...], axis=0)


def on_device(dp_n, nf, layer_in, in_b, in_c, dt_raw, a_log, skip_gain, dt_bias, foot_map, contact, out_grad):
    chips = nf // 2
    lanes = HP // (chips // 8)
    vm = lambda *shape: pltpu.VMEM(shape, F32)
    vb = lambda *shape: pltpu.VMEM(shape, BF16)
    whole = pl.BlockSpec(memory_space=pltpu.VMEM)
    gx, gb, gc, gdt, hg = pl.pallas_call(
        functools.partial(kernel, dp_n, nf),
        out_shape=(
            jax.ShapeDtypeStruct((T, HP), BF16),
            jax.ShapeDtypeStruct((T, N), F32),
            jax.ShapeDtypeStruct((T, N), F32),
            jax.ShapeDtypeStruct((H, T), F32),
            jax.ShapeDtypeStruct((8, 128), F32),
        ),
        in_specs=[whole] * 10,
        out_specs=[whole] * 5,
        scratch_shapes=[
            vm(N, HP),
            vm(N, HP),
            vm(N, HP),
            vm(N, HP),
            vm(N // 2, HP),
            vm(N // 2, HP),
            vm(chips, 8, lanes),
            vm(chips, 8, lanes),
            vm(chips, 8, lanes),
            vm(chips, 8, lanes),
            vm(N, HP),
            vm(N, HP),
            vm(T, HP),
            vm(T, HP),
            vm(T, HP),
            vm(T, HP),
            vb(T, HP),
            vb(T, HP),
            vb(T, HP),
            vb(T, HP),
            vm(128, HP),
            vm(PAIRS, 8, T),
            vm(H, T),
            vm(H, T),
            vm(T, T),
            vm(T, T),
            vm(128, T),
            vm(128, 128),
            vm(8, 128),
            vm(nf, 8, 128),
            vm(8, 128),
            vm(nf, 128),
            vm(T, 128),
            vm(8, 128),
            vm(8, 128),
            vm(N, KL),
            vm(nf, 8, 128),
            vm(nf, 8, 128),
            vm(N, KL),
            vm(H, T),
            vm(H, T),
            vm(8, HP),
            vm(8, HP),
            vm(8, 128),
            vm(G1, 8, 128),
            vm(8, 128),
            vm(dp_n * (nf // G1), 8, 128),
            pltpu.SemaphoreType.DMA((18,)),
            pltpu.SemaphoreType.DMA((18,)),
        ],
        compiler_params=pltpu.CompilerParams(
            collective_id=0, has_side_effects=True, vmem_limit_bytes=56 * 2**20
        ),
    )(
        layer_in[0],
        in_b[0],
        in_c[0],
        dt_raw[0],
        a_log[None],
        skip_gain[None],
        dt_bias[None],
        foot_map,
        contact,
        out_grad[0],
    )
    return gx[None], gb[None], gc[None], gdt[None], hg[0:3, 0:H]


def solution(mesh):
    return jax.shard_map(
        functools.partial(on_device, mesh.shape["dp"], mesh.shape["frame"]),
        mesh=mesh,
        in_specs=(
            P("dp", "frame", None),
            P("dp", "frame", None),
            P("dp", "frame", None),
            P("dp", None, "frame"),
            P(),
            P(),
            P(),
            P(),
            P("dp", "frame"),
            P("dp", "frame", None),
        ),
        out_specs=(
            P("dp", "frame", None),
            P("dp", "frame", None),
            P("dp", "frame", None),
            P("dp", None, "frame"),
            P(),
        ),
        check_vma=False,
    )
```

time: 1050 us -> 133 us (0.13); the launches traced: 1030 us -> 133 us
  waiting for transfers between devices: 318 us -> 0 us
  other arithmetic: 212 us -> 0 us
  blocking collectives: 208 us -> 0 us
  local copies, waits for them, and re-layouts: 170 us -> 5.91 us
  Pallas kernels: 0 us -> 126 us
  matrix products: 88 us -> 0 us
  loops' own time: 16.1 us -> 0 us
  between operations: 15.2 us -> 0.66 us
    all_gather x2 -> x0, waiting for transfers between devices: 316 us -> none  [carried_in(): everything = jax.tree.map(lambda part: lax.all_gather(part, axis), array)]
    select_n x128 -> x0, other arithmetic: 187 us -> none  [hop(): return jax.tree.map(lambda a, b: jnp.where(reached, a, b), new, before)]
    unnamed x1 -> x0, blocking collectives: 133 us -> none
    pallas_call x0 -> x1, Pallas kernels: none -> 126 us  [on_device(): pl.pallas_call(functools.partial(kernel, dp_n, nf), out_shape=(jax.ShapeD...]
    dot_general x42 -> x0, matrix products: 88 us -> none  [the longest x6 29.1 us: group_pass(): inner = jnp.einsum('hts,shp->thp', mixing, block_x, precision=HIGH)]
    psum x1 -> x0, blocking collectives: 74.3 us -> none  [on_device(): lax.psum(jnp.stack([grad_log, grad_skip, grad_bias]), ('dp', 'frame'))]
    mul x131 -> x0, local copies, waits for them, and re-layouts: 52.6 us -> none  [the longest x128 45.2 us: combine_states(): later[0][:, None, None] * earlier[1] + later[1]]
    dynamic_update_slice x4 -> x0, local copies, waits for them, and re-layouts: 52 us -> none  [run_blocks(): lax.scan(jax.checkpoint(advance), state, (block_x, block_b, block_c, bloc...]
  transfers between devices with their start and end apart: 4 -> 0, of which waited for: 3 -> 0; matrix products, arithmetic and copies ran while one was open for 3% -> 0% of each run, Pallas kernels for 0% -> 0%
where the time goes in v1:
time: 133 us
  Pallas kernels  126 us (95%)
  local copies, waits for them, and re-layouts  5.91 us (4%)
    pallas_call x1, Pallas kernels, on_device(): pl.pallas_call(functools.partial(kernel, dp_n, nf), out_shape=(jax.ShapeD...  126 us
    unnamed x12, local copies, waits for them, and re-layouts  5.33 us

profile of v1, /device:TPU:1, one launch (start us, length us, event | category | flops | bytes accessed | tf_op | source)
XLA Modules:
  0.0 132.8 jit_solution(5580934698101128629)
XLA Ops:
  0.6 126.2 %shard_map.137 = (bf16[256,2048]{1,0:T(8,128)(2,1)}, f32[256,128]{1,0:T(8,128)}, f32[256,128]{1,0:T(8,128)}, f32[32,256]{1,0:T(8,128)}, f32[8,128]{1,0:T(8,128)}) custom-call(bf16[256,2048]{1,0:T(8,128)(2,1)} %bitcast.12, bf16[256,128]{1,0:T(8,128)(2,1)} %bitcast.17, bf16[256,128]{1,0:T(8,128)(2,1)} %bitcast.18, f32[32,256]{1,0:T(8,128)} %bitcast.19, ...), custom_call_target="tpu_custom_call" | custom-call | tf_op jit(solution)/shard_map/pallas_call | solution.py:579
  126.8 0.0 copy-start.3
  126.9 0.7 copy-done.3
  127.5 0.6 slice.3
  128.1 0.0 copy-start.1
  128.1 2.3 %copy.19 = bf16[1,256,2048]{2,1,0:T(8,128)(2,1)} copy(bf16[1,256,2048]{2,1,0:T(8,128)(2,1)} %bitcast.14) | data formatting | bytes 2097152
  130.4 0.0 copy-done.1
  130.4 0.0 copy-start
  130.4 0.7 copy.20
  131.1 0.3 copy-done
  131.4 0.0 copy-start.2
  131.4 0.7 copy.21
  132.1 0.1 copy-done.2
  132.2 0.6 copy.22
Async XLA Ops:
  126.8 0.7 copy-start.3
  128.1 2.3 %copy-start.1 = (f32[256,128]{1,0:T(8,128)S(1)}, f32[256,128]{1,0:T(8,128)}, u32[]{:S(2)}) copy-start(f32[256,128]{1,0:T(8,128)} %get-tuple-element.11) | copy-start | bytes 393220
  130.4 1.0 copy-start
  131.4 0.8 copy-start.2

commit v2 on v1

--- a/solution.py
+++ b/solution.py
@@ -14,6 +14,8 @@
 PAIRS = HP // 128
 LOG2E = 1.4426950408889634
 KL = 512
+WB = 256
+BLOCKS = HP // WB
 G1 = 16
 
 
@@ -91,15 +93,24 @@
     zlo,
     dyhi,
     dylo,
-    fpad,
+    whi,
+    wlo,
+    bhi,
+    blo,
+    f48,
+    e96,
+    row_sk,
+    row_sib,
     c2_ref,
     ld_ref,
+    step_ref,
     sg_ref,
     sc_ref,
     sct_ref,
     ds0,
     ds1,
     dec_mine,
+    dec_row,
     decs,
     sib_dec,
     dec_all,
@@ -107,6 +118,8 @@
     vel_prev,
     vel_next,
     gd_local,
+    gd_sib,
+    gd_half,
     gd_got,
     gd_ret,
     gd_end,
@@ -129,29 +142,38 @@
     first = core == 0
     lbs = chips // 8
     lanes = HP // lbs
-    g2n = dp_n * (nf // G1)
+    halves = chips // G1
+    g2n = dp_n * halves * 2
+    group, low = chip // G1, chip % G1
+    spot = (me_dp * halves + group) * 2 + core
 
     def ring(k, base=None):
         return lax.rem(me + k, nf)
 
     barrier = pltpu.get_barrier_semaphore()
 
-    @pl.loop(1, nf)
-    def _(k):
-        pl.semaphore_signal(barrier, inc=1, device_id=(me_dp, ring(k)), device_id_type=MESH)
-
-    group = me // G1
-    low = me % G1
-
-    @pl.loop(1, dp_n)
-    def _(k):
-        d = lax.rem(me_dp + k, dp_n)
-
-        @pl.loop(0, nf // G1)
-        def _(j):
-            pl.semaphore_signal(
-                barrier, inc=1, device_id=(d, j * G1 + low), device_id_type=MESH
-            )
+    def greet(frame, dp=None):
+        pl.semaphore_signal(
+            barrier,
+            inc=1,
+            device_id=(me_dp if dp is None else dp, frame),
+            device_id_type=MESH,
+        )
+
+    def second(k):
+        j = lax.rem(spot + k, g2n)
+        return (j // 2 % halves * G1 + low) * 2 + j % 2, j // (2 * halves)
+
+    greet(sib)
+    greet(lax.rem(me + nf - 1 + 2 * core, nf))
+
+    @pl.loop(1, chips)
+    def _(k):
+        greet(lax.rem(chip + k, chips) * 2 + core)
+
+    @pl.loop(1, g2n)
+    def _(k):
+        greet(*second(k))
 
     def remote(src, dst, s, r, dev, dp=None):
         return pltpu.make_async_remote_copy(
@@ -163,6 +185,11 @@
             device_id_type=MESH,
         )
 
+    def arrived(buf, n, s):
+        view = buf.at[pl.ds(0, n)]
+        d = remote(view, view, s, s, sib)
+        d.wait()
+
     eye = (iota((T, T), 0) == iota((T, T), 1)).astype(F32)
     rows8 = iota((8, H), 0)
     rows = jnp.where(
@@ -177,6 +204,7 @@
     sg_ref[...] = jnp.where(raw >= 0, 1.0, tail) / (1.0 + tail)
     ld = rate * step
     ld_ref[...] = ld
+    step_ref[...] = step
     upper = (iota((T, T), 0) <= iota((T, T), 1)).astype(F32)
     c2 = nn_hi(ld, upper) * LOG2E
     for i in range(PAIRS):
@@ -191,13 +219,19 @@
     bt = nt(eye_b, bb).astype(BF16)
     ct = nt(eye_b, cc).astype(BF16)
 
-    fpad[...] = jnp.zeros_like(fpad)
-    fpad[0:FEET, :] = f_ref[...]
-
-    @pl.loop(0, PAIRS)
+    fhi, flo = split(jnp.concatenate([f_ref[...], jnp.zeros((4, HP), F32)], axis=0))
+    f48[...] = jnp.concatenate([fhi, flo, fhi], axis=0)
+    e96[...] = (iota((96, HP), 0) % H == iota((96, HP), 1) // PS).astype(BF16)
+    sk8 = jnp.broadcast_to(sk_ref[...], (8, H))
+    row_sk[...] = nn(jnp.concatenate(split3(sk8), axis=1), e96[...])
+
+    def block(i):
+        return pl.ds(pl.multiple_of(i * WB, WB), WB)
+
+    @pl.loop(0, BLOCKS, unroll=2)
     def _(i):
-        blk = pl.ds(pl.multiple_of(i * 128, 128), 128)
-        e3 = (iota((96, 128), 0) % H == 2 * i + iota((96, 128), 1) // PS).astype(BF16)
+        blk = block(i)
+        e3 = e96[:, blk]
         cb, sb = nn(c3, e3), nn(s3, e3)
         cexp[:, blk] = cb
         sexp[:, blk] = sb
@@ -206,11 +240,11 @@
         zhi[:, blk] = hi
         zlo[:, blk] = lo
         hi, lo = split(jnp.exp2(cb[T - 1 : T] - cb) * z)
+        whi[:, blk] = hi
+        wlo[:, blk] = lo
         local_f[:, blk] = nn(bt, hi) + nn(bt, lo)
-        hi, lo = split(jnp.exp2(cb) * og_ref[:, blk].astype(F32))
-        local_r[:, blk] = nn(ct, hi) + nn(ct, lo)
-
-    pl.semaphore_wait(barrier, nf - 1 + (dp_n - 1) * (nf // G1))
+
+    pl.semaphore_wait(barrier, chips + g2n)
 
     mine_half = pl.ds(pl.multiple_of(core * 64, 64), 64)
     sib_half = pl.ds(pl.multiple_of(64 - core * 64, 64), 64)
@@ -223,60 +257,61 @@
     ]
     ex_dec.start()
     ex[0].start()
-    ex[1].start()
-
-    @pl.loop(1, nf)
-    def _(k):
-        remote(dec_mine, decs.at[me], 0, 0, ring(k)).start()
-
-    decs[me] = dec_mine[...]
-
-    scores = nt(cc, bb)
-    sc_ref[...] = jnp.where(iota((T, T), 0) >= iota((T, T), 1), scores, 0.0)
-    scores = nt(bb, cc)
-    sct_ref[...] = jnp.where(iota((T, T), 0) <= iota((T, T), 1), scores, 0.0)
-
-    def sib_decay(i):
-        e1 = (iota((128, 128), 0) == 2 * i + iota((128, 128), 1) // PS).astype(F32)
-        return jnp.exp2(nn_hi(sib_dec[...], e1))[0:1]
-
+
+    def reverse(i):
+        blk = block(i)
+        hi, lo = split(jnp.exp2(cexp[:, blk]) * og_ref[:, blk].astype(F32))
+        local_r[:, blk] = nn(ct, hi) + nn(ct, lo)
+
+    pl.loop(0, BLOCKS // 2, unroll=2)(reverse)
     ex_dec.wait()
+    row_sib[...] = jnp.exp2(
+        nn(jnp.concatenate(split3(sib_dec[:, 0:H]), axis=1), e96[...])
+    )
     ex[0].wait()
-    ex[1].wait()
-
-    @pl.loop(0, PAIRS)
+
+    def part(o):
+        return (
+            pl.ds(pl.multiple_of(o // lbs * 8, 8), 8),
+            pl.ds(pl.multiple_of(o % lbs * lanes, 128), lanes),
+        )
+
+    my_r, my_l = part(chip)
+
+    @pl.loop(0, BLOCKS)
     def _(i):
-        blk = pl.ds(pl.multiple_of(i * 128, 128), 128)
-        d_sib = sib_decay(i)
-        d_me = jnp.exp2(cexp[pl.ds(T - 8, 8), blk])[7:8]
+        blk = block(i)
+        d_sib = row_sib[0:1, blk]
+        d_me = jnp.exp2(cexp[T - 8 : T, blk])[7:8]
         one = jnp.ones_like(d_me)
         half_f[:, blk] = (
             jnp.where(first, d_sib, one) * local_f[mine_half, blk]
             + jnp.where(first, one, d_me) * sib_f[mine_half, blk]
         )
-        half_r[:, blk] = (
-            jnp.where(first, one, d_sib) * local_r[mine_half, blk]
-            + jnp.where(first, d_me, one) * sib_r[mine_half, blk]
-        )
-
-    def part(o):
-        return (
-            pl.ds(pl.multiple_of(o // lbs * 8, 8), 8),
-            pl.ds(pl.multiple_of(o % lbs * lanes, 128), lanes),
-        )
 
     @pl.loop(1, chips)
     def _(k):
         o = lax.rem(chip + k, chips)
         r, l = part(o)
         remote(half_f.at[r, l], got_f.at[chip], 6, 6, o * 2 + core).start()
-        remote(half_r.at[r, l], got_r.at[chip], 7, 7, o * 2 + core).start()
-
+
+    got_f[chip] = half_f[my_r, my_l]
+    dec_row[...] = dec_mine[0:1] + sib_dec[0:1]
+    decs[chip] = dec_row[...]
+    pl.loop(BLOCKS // 2, BLOCKS, unroll=2)(reverse)
+    ex[1].start()
     ex[2].start()
     ex[3].start()
-    my_r, my_l = part(chip)
-    got_f[chip] = half_f[my_r, my_l]
-    got_r[chip] = half_r[my_r, my_l]
+
+    @pl.loop(1, chips)
+    def _(k):
+        o = lax.rem(chip + k, chips)
+        remote(dec_row, decs.at[chip], 0, 0, o * 2 + core).start()
+
+    scores = nt(cc, bb)
+    sc_ref[...] = jnp.where(iota((T, T), 0) >= iota((T, T), 1), scores, 0.0)
+    scores = nt(bb, cc)
+    sct_ref[...] = jnp.where(iota((T, T), 0) <= iota((T, T), 1), scores, 0.0)
 
     low_lanes = iota((128, 128), 1) < PS
 
@@ -297,21 +332,29 @@
                 outs.append(res[:, 0:128] + res[:, 128:256])
             yv[at, blk] = jnp.where(low_lanes, outs[0], outs[1])
 
-    pl.loop(0, PAIRS // 2)(inner)
-
-    def arrived(buf, n, s):
-        view = buf.at[pl.ds(0, n)]
-        d = remote(view, view, s, s, sib)
-        d.wait()
-
-    arrived(decs, nf - 1, 0)
+    pl.loop(0, 3)(inner)
+    ex[1].wait()
+
+    @pl.loop(0, BLOCKS)
+    def _(i):
+        blk = block(i)
+        d_sib = row_sib[0:1, blk]
+        d_me = jnp.exp2(cexp[T - 8 : T, blk])[7:8]
+        one = jnp.ones_like(d_me)
+        half_r[:, blk] = (
+            jnp.where(first, one, d_sib) * local_r[mine_half, blk]
+            + jnp.where(first, d_me, one) * sib_r[mine_half, blk]
+        )
+
+    got_r[chip] = half_r[my_r, my_l]
+
+    pl.loop(3, 9)(inner)
+    arrived(decs, chips - 1, 0)
     dall = decs[:, 0, :]
     dec_all[...] = jnp.exp2(dall)
-    pairsum = (iota((chips, nf), 0) == iota((chips, nf), 1) // 2).astype(F32)
-    chip_log = nn_hi(pairsum, dall)
     head0 = chip % lbs * (lanes // PS)
     spread_l = (iota((128, lanes), 0) == head0 + iota((128, lanes), 1) // PS).astype(F32)
-    chip_dec = jnp.exp2(nn_hi(chip_log, spread_l))
+    chip_dec = jnp.exp2(nn_hi(dall, spread_l))
 
     arrived(got_f, chips - 1, 6)
     acc = jnp.zeros((8, lanes), F32)
@@ -325,49 +368,48 @@
         r = pl.ds(pl.multiple_of(core * 64 + chip // lbs * 8, 8), 8)
         remote(ret_f.at[o], s_in.at[r, my_l], 8, 8, o * 2 + core).start()
 
-    arrived(got_r, chips - 1, 7)
-    acc = jnp.zeros((8, lanes), F32)
-    for q in reversed(range(chips)):
-        ret_r[q] = acc
-        acc = got_r[q] + chip_dec[q : q + 1] * acc
-
-    @pl.loop(1, chips)
-    def _(k):
-        o = lax.rem(chip + k, chips)
-        r = pl.ds(pl.multiple_of(core * 64 + chip // lbs * 8, 8), 8)
-        remote(ret_r.at[o], g_end.at[r, my_l], 9, 9, o * 2 + core).start()
-
     own = pl.ds(pl.multiple_of(core * 64 + chip // lbs * 8, 8), 8)
     s_in[own, my_l] = ret_f[chip]
-    g_end[own, my_l] = ret_r[chip]
-
-    pl.loop(PAIRS // 2, PAIRS)(inner)
-
+    pl.loop(9, PAIRS)(inner)
+
+    @pl.loop(0, BLOCKS)
+    def _(i):
+        blk = block(i)
+        eh = e96[0:H, blk]
+        fhi, flo = f48[0:16, blk], f48[16:32, blk]
+        for k in range(FEET):
+            rows_k = slice(k * H, k * H + H)
+            bhi[rows_k, blk] = jnp.where(eh > 0, jnp.broadcast_to(fhi[k : k + 1], eh.shape), 0.0).astype(BF16)
+            blo[rows_k, blk] = jnp.where(eh > 0, jnp.broadcast_to(flo[k : k + 1], eh.shape), 0.0).astype(BF16)
+
+    ex[2].wait()
+    ex[3].wait()
     arrived(ret_f, chips - 1, 8)
     back_f = remote(s_in.at[mine_half], s_in.at[mine_half], 10, 10, sib)
     back_f.start()
-    ex[2].wait()
-    ex[3].wait()
+
+    @pl.loop(1, chips)
+    def _(k):
+        o = lax.rem(chip + k, chips)
+        r, l = part(o)
+        remote(half_r.at[r, l], got_r.at[chip], 7, 7, o * 2 + core).start()
+
     back_f.wait()
 
     vel[...] = jnp.zeros_like(vel)
-    sk8 = jnp.broadcast_to(sk_ref[...], (8, H))
-
-    @pl.loop(0, PAIRS)
+
+    @pl.loop(0, BLOCKS, unroll=2)
     def _(i):
-        blk = pl.ds(pl.multiple_of(i * 128, 128), 128)
-        d_sib = sib_decay(i)
+        blk = block(i)
         state = s_in[:, blk]
-        state = jnp.where(first, state, sib_f[:, blk] + d_sib * state)
+        state = jnp.where(first, state, sib_f[:, blk] + row_sib[0:1, blk] * state)
         s_in[:, blk] = state
         hi, lo = split(state)
         y = yv[:, blk] + jnp.exp2(cexp[:, blk]) * (nn(cc, hi) + nn(cc, lo))
         yv[:, blk] = y
-        e1 = (iota((H, 128), 0) == 2 * i + iota((H, 128), 1) // PS).astype(F32)
-        out = y + nn_hi(sk8, e1)[0:1] * x_ref[:, blk].astype(F32)
-        hi, lo = split(out)
-        fhi, flo = split(fpad[:, blk])
-        vel[...] += nt(hi, fhi) + nt(lo, fhi) + nt(hi, flo)
+        hi, lo = split(y + row_sk[0:1, blk] * x_ref[:, blk].astype(F32))
+        both = nt(hi, f48[0:32, blk])
+        vel[:, 0:16] += both[:, 0:16] + both[:, 16:32] + nt(lo, f48[0:16, blk])
 
     touch = jnp.broadcast_to(ct_ref[...].astype(F32), (8, T))
     touch = nt_hi(eye, touch)[:, 0:1]
@@ -396,33 +438,56 @@
     hi, lo = split(jnp.exp2(c_feet) * (nn(chi, feet_of) + nn(clo, feet_of)))
     gd_local[...] = nn(ct, hi) + nn(ct, lo)
 
-    def tile(o):
+    gd_ex = remote(gd_local, gd_sib, 18, 18, sib)
+    gd_ex.start()
+
+    def tile(o, base):
         return (
-            pl.ds(pl.multiple_of(o // 4 * 8, 8), 8),
+            pl.ds(pl.multiple_of(base + o // 4 * 8, 8), 8),
             pl.ds(pl.multiple_of(o % 4 * 128, 128), 128),
         )
 
-    @pl.loop(1, nf)
-    def _(k):
-        o = ring(k)
-        r, l = tile(o)
-        remote(gd_local.at[r, l], gd_got.at[me], 14, 14, o).start()
-
-    my_tr, my_tl = tile(me)
-    gd_got[me] = gd_local[my_tr, my_tl]
-
-    arrived(ret_r, chips - 1, 9)
-    back_r = remote(g_end.at[mine_half], g_end.at[mine_half], 11, 11, sib)
-    back_r.start()
-
-    @pl.loop(0, PAIRS)
-    def _(i):
-        blk = pl.ds(pl.multiple_of(i * 128, 128), 128)
-        fhi, flo = split(fpad[:, blk])
-        dy = og_ref[:, blk].astype(F32) + nn(chi, fhi) + nn(clo, fhi) + nn(chi, flo)
-        hi, lo = split(dy)
+    c48 = jnp.concatenate([chi[:, 0:16], chi[:, 0:16], clo[:, 0:16]], axis=1)
+
+    def total_grad(i):
+        blk = block(i)
+        hi, lo = split(og_ref[:, blk].astype(F32) + nn(c48, f48[:, blk]))
         dyhi[:, blk] = hi
         dylo[:, blk] = lo
+
+    pl.loop(0, BLOCKS // 2, unroll=2)(total_grad)
+    gd_ex.wait()
+    decay_me = jnp.exp2(jnp.concatenate([dec_mine[0:1]] * 4, axis=1))
+    decay_sib = jnp.exp2(jnp.concatenate([sib_dec[0:1]] * 4, axis=1))
+    one = jnp.ones_like(decay_me)
+    gd_half[...] = (
+        jnp.where(first, one, decay_sib) * gd_local[mine_half, :]
+        + jnp.where(first, decay_me, one) * gd_sib[mine_half, :]
+    )
+
+    @pl.loop(1, chips)
+    def _(k):
+        o = lax.rem(chip + k, chips)
+        r, l = tile(o, 0)
+        remote(gd_half.at[r, l], gd_got.at[chip], 14, 14, o * 2 + core).start()
+
+    gd_r, gd_l = tile(chip, 0)
+    gd_got[chip] = gd_half[gd_r, gd_l]
+    gd_r, gd_l = tile(chip, core * 64)
+    pl.loop(BLOCKS // 2, BLOCKS, unroll=2)(total_grad)
+    arrived(got_r, chips - 1, 7)
+    acc = jnp.zeros((8, lanes), F32)
+    for q in reversed(range(chips)):
+        ret_r[q] = acc
+        acc = got_r[q] + chip_dec[q : q + 1] * acc
+
+    @pl.loop(1, chips)
+    def _(k):
+        o = lax.rem(chip + k, chips)
+        r = pl.ds(pl.multiple_of(core * 64 + chip // lbs * 8, 8), 8)
+        remote(ret_r.at[o], g_end.at[r, my_l], 9, 9, o * 2 + core).start()
+
+    g_end[own, my_l] = ret_r[chip]
 
     ds0[...] = jnp.zeros_like(ds0)
     ds1[...] = jnp.zeros_like(ds1)
@@ -453,22 +518,21 @@
             acc[...] = total
             dz[at, blk] = jnp.where(low_lanes, outs[0], outs[1])
 
-    pl.loop(0, PAIRS // 2)(backward)
-
-    arrived(gd_got, nf - 1, 14)
+    pl.loop(0, 5)(backward)
+
+    arrived(gd_got, chips - 1, 14)
     acc = jnp.zeros((8, 128), F32)
-    for q in reversed(range(nf)):
+    for q in reversed(range(chips)):
         gd_ret[q] = acc
         acc = gd_got[q] + dec_all[q : q + 1] * acc
 
-    @pl.loop(1, nf)
-    def _(k):
-        o = ring(k)
-        remote(gd_ret.at[o], gd_end.at[my_tr, my_tl], 15, 15, o).start()
-
-    gd_end[my_tr, my_tl] = gd_ret[me]
-
-    pl.loop(PAIRS // 2, PAIRS)(backward)
+    @pl.loop(1, chips)
+    def _(k):
+        o = lax.rem(chip + k, chips)
+        remote(gd_ret.at[o], gd_end.at[gd_r, gd_l], 15, 15, o * 2 + core).start()
+
+    gd_end[gd_r, gd_l] = gd_ret[chip]
+    pl.loop(5, PAIRS)(backward)
 
     m0 = iota((128, T), 0) <= iota((128, T), 1)
     m1 = iota((128, 128), 0) <= iota((128, 128), 1)
@@ -483,63 +547,63 @@
     )
     hi, lo = split(dst)
     gb_ref[...] = nn(hi, cc) + nn(lo, cc)
+    p1[...] = jnp.zeros_like(p1)
     eye_t = eye.astype(BF16)
     hi = nt(eye_t, hi).astype(BF16)
     lo = nt(eye_t, lo).astype(BF16)
     gc_ref[...] = nn(hi, bb) + nn(lo, bb)
 
-    @pl.loop(0, PAIRS)
+    @pl.loop(0, BLOCKS, unroll=2)
     def _(i):
-        blk = pl.ds(pl.multiple_of(i * 128, 128), 128)
+        blk = block(i)
         dy = dyhi[:, blk].astype(F32) + dylo[:, blk].astype(F32)
         hi, lo = split(jnp.exp2(cexp[:, blk]) * dy)
         shi, slo = split(s_in[:, blk])
         gc_ref[...] += nt(hi, shi) + nt(lo, shi) + nt(hi, slo)
-
+        x = x_ref[:, blk].astype(F32)
+        hi, lo = split(yv[:, blk] * dy)
+        eh = e96[0:H, blk]
+        p1[...] += nt(eh, hi) + nt(eh, lo)
+        row_d[:, blk] = jnp.broadcast_to(jnp.sum(x * dy, axis=0, keepdims=True), (8, WB))
+
+    arrived(ret_r, chips - 1, 9)
+    back_r = remote(g_end.at[mine_half], g_end.at[mine_half], 11, 11, sib)
+    back_r.start()
+    arrived(gd_ret, chips - 1, 15)
+    gd_back = remote(gd_end.at[mine_half], gd_end.at[mine_half], 19, 19, sib)
+    gd_back.start()
+    gd_back.wait()
     back_r.wait()
-    view = gd_ret.at[pl.ds(0, nf - 1)]
-    remote(view, view, 15, 15, sib).wait()
-
-    p1[...] = jnp.zeros_like(p1)
+
     p2[...] = jnp.zeros_like(p2)
-    gdh, gdl = split(gd_end[:, 0 : FEET * H])
-
-    @pl.loop(0, PAIRS)
+    gd_all = gd_end[...]
+    gd_all = jnp.where(first, gd_sib[...] + decay_sib * gd_all, gd_all)
+    gdh, gdl = split(gd_all[:, 0 : FEET * H])
+
+    @pl.loop(0, BLOCKS, unroll=2)
     def _(i):
-        blk = pl.ds(pl.multiple_of(i * 128, 128), 128)
-        here = iota((H, 128), 0) == 2 * i + iota((H, 128), 1) // PS
-        e1 = here.astype(F32)
-        e1b = here.astype(BF16)
-        ff = fpad[0:16, blk]
-        big = jnp.concatenate([ff[k : k + 1] * e1 for k in range(FEET)], axis=0)
-        bhi, blo = split(big)
+        blk = block(i)
+        eh = e96[0:H, blk]
         grad = g_end[:, blk]
-        grad = jnp.where(first, sib_r[:, blk] + sib_decay(i) * grad, grad)
-        grad = grad + nn(gdh, bhi) + nn(gdl, bhi) + nn(gdh, blo)
+        grad = jnp.where(first, sib_r[:, blk] + row_sib[0:1, blk] * grad, grad)
+        grad = grad + nn(gdh, bhi[:, blk]) + nn(gdl, bhi[:, blk]) + nn(gdh, blo[:, blk])
+        g_end[:, blk] = grad
         ghi, glo = split(grad)
-        cb, sb = cexp[:, blk], sexp[:, blk]
+        cb = cexp[:, blk]
         last = cb[T - 1 : T]
-        fade = jnp.exp2(last - cb)
-        x = x_ref[:, blk].astype(F32)
-        dzb = dz[:, blk] + fade * (nn(bb, ghi) + nn(bb, glo))
-        dy = dyhi[:, blk].astype(F32) + dylo[:, blk].astype(F32)
-        gx_ref[:, blk] = (nn_hi(sk8, e1)[0:1] * dy + sb * dzb).astype(BF16)
-        xdz = x * dzb
+        dzb = dz[:, blk] + jnp.exp2(last - cb) * (nn(bb, ghi) + nn(bb, glo))
+        dz[:, blk] = dzb
+        xdz = x_ref[:, blk].astype(F32) * dzb
         hi, lo = split(xdz)
-        p2[...] += nt(e1b, hi) + nt(e1b, lo)
-        hi, lo = split(yv[:, blk] * dy - sb * xdz)
-        p1[...] += nt(e1b, hi) + nt(e1b, lo)
-        hi, lo = split(fade * sb * x)
-        gb_ref[...] += nt(hi, ghi) + nt(lo, ghi) + nt(hi, glo)
+        p2[...] += nt(eh, hi) + nt(eh, lo)
         s_last = jnp.exp2(last) * s_in[:, blk] + local_f[:, blk]
-        row_d[:, blk] = jnp.broadcast_to(jnp.sum(x * dy, axis=0, keepdims=True), (8, 128))
-        row_b[:, blk] = jnp.broadcast_to(jnp.sum(grad * s_last, axis=0, keepdims=True), (8, 128))
+        row_b[:, blk] = jnp.broadcast_to(jnp.sum(grad * s_last, axis=0, keepdims=True), (8, WB))
 
     heads = (iota((H, HP), 0) == iota((H, HP), 1) // PS).astype(F32)
     edge_h = nt_hi(heads, row_b[...])[:, 0:1]
     skip_h = nt_hi(row_d[...], heads)
     later = (iota((T, T), 0) >= iota((T, T), 1)).astype(F32)
-    dld = nn_hi(p1[...], later) + edge_h
+    dld = nn_hi(p1[...] - step_ref[...] * p2[...], later) + edge_h
     gdt = (rate * dld + p2[...]) * sg_ref[...]
     gdt_ref[...] = gdt
     ones8 = jnp.ones((8, T), F32)
@@ -551,23 +615,43 @@
     @pl.loop(1, G1)
     def _(k):
         j = lax.rem(low + k, G1)
-        remote(hsum, hgot1.at[low], 16, 16, group * G1 + j).start()
+        remote(hsum, hgot1.at[low], 16, 16, (group * G1 + j) * 2 + core).start()
 
     hgot1[low] = hsum[...]
+
+    def sources(i):
+        blk = block(i)
+        dy = dyhi[:, blk].astype(F32) + dylo[:, blk].astype(F32)
+        gx_ref[:, blk] = (row_sk[0:1, blk] * dy + sexp[:, blk] * dz[:, blk]).astype(BF16)
+        hi, lo = whi[:, blk], wlo[:, blk]
+        ghi, glo = split(g_end[:, blk])
+        gb_ref[...] += nt(hi, ghi) + nt(lo, ghi) + nt(hi, glo)
+
+    pl.loop(0, BLOCKS // 2, unroll=2)(sources)
     arrived(hgot1, G1 - 1, 16)
     hmid[...] = jnp.sum(hgot1[...], axis=0)
-    spot = me_dp * (nf // G1) + group
 
     @pl.loop(1, g2n)
     def _(k):
-        j = lax.rem(spot + k, g2n)
-        remote(
-            hmid, hgot2.at[spot], 17, 17, j % (nf // G1) * G1 + low, j // (nf // G1)
-        ).start()
+        frame, dp = second(k)
+        remote(hmid, hgot2.at[spot], 17, 17, frame, dp).start()
 
     hgot2[spot] = hmid[...]
+    pl.loop(BLOCKS // 2, BLOCKS, unroll=2)(sources)
     arrived(hgot2, g2n - 1, 17)
     hg_ref[...] = jnp.sum(hgot2[...], axis=0)
+
+
+def hand_out(gx, gb, gc, gdt, hg, gx_o, gb_o, gc_o, gdt_o, hg_o, sem):
+    pairs = ((gx, gx_o), (gb, gb_o), (gc, gc_o), (gdt, gdt_o))
+    copies = [
+        pltpu.make_async_copy(a, b.at[0], sem.at[k]) for k, (a, b) in enumerate(pairs)
+    ]
+    for copy in copies:
+        copy.start()
+    hg_o[...] = hg[0:3, 0:H]
+    for copy in copies:
+        copy.wait()
 
 
 def on_device(dp_n, nf, layer_in, in_b, in_c, dt_raw, a_log, skip_gain, dt_bias, foot_map, contact, out_grad):
@@ -608,8 +692,16 @@
             vb(T, HP),
             vb(T, HP),
             vb(T, HP),
-            vm(128, HP),
+            vb(T, HP),
+            vb(T, HP),
+            vb(FEET * H, HP),
+            vb(FEET * H, HP),
+            vb(48, HP),
+            vb(96, HP),
+            vm(8, HP),
+            vm(8, HP),
             vm(PAIRS, 8, T),
+            vm(H, T),
             vm(H, T),
             vm(H, T),
             vm(T, T),
@@ -617,15 +709,18 @@
             vm(128, T),
             vm(128, 128),
             vm(8, 128),
-            vm(nf, 8, 128),
+            vm(1, 128),
+            vm(chips, 1, 128),
             vm(8, 128),
-            vm(nf, 128),
+            vm(chips, 128),
             vm(T, 128),
             vm(8, 128),
             vm(8, 128),
             vm(N, KL),
-            vm(nf, 8, 128),
-            vm(nf, 8, 128),
+            vm(N, KL),
+            vm(N // 2, KL),
+            vm(chips, 8, 128),
+            vm(chips, 8, 128),
             vm(N, KL),
             vm(H, T),
             vm(H, T),
@@ -635,8 +730,8 @@
             vm(G1, 8, 128),
             vm(8, 128),
             vm(dp_n * (nf // G1), 8, 128),
-            pltpu.SemaphoreType.DMA((18,)),
-            pltpu.SemaphoreType.DMA((18,)),
+            pltpu.SemaphoreType.DMA((20,)),
+            pltpu.SemaphoreType.DMA((20,)),
         ],
         compiler_params=pltpu.CompilerParams(
             collective_id=0, has_side_effects=True, vmem_limit_bytes=56 * 2**20
@@ -653,7 +748,20 @@
         contact,
         out_grad[0],
     )
-    return gx[None], gb[None], gc[None], gdt[None], hg[0:3, 0:H]
+    place = pl.BlockSpec(memory_space=pl.ANY)
+    return pl.pallas_call(
+        hand_out,
+        out_shape=(
+            jax.ShapeDtypeStruct((1, T, HP), BF16),
+            jax.ShapeDtypeStruct((1, T, N), F32),
+            jax.ShapeDtypeStruct((1, T, N), F32),
+            jax.ShapeDtypeStruct((1, H, T), F32),
+            jax.ShapeDtypeStruct((3, H), F32),
+        ),
+        in_specs=[whole] * 5,
+        out_specs=[place] * 4 + [whole],
+        scratch_shapes=[pltpu.SemaphoreType.DMA((4,))],
+    )(gx, gb, gc, gdt, hg)
 
 
 def solution(mesh):

time: 133 us -> 104 us (0.78)
  Pallas kernels: 126 us -> 103 us
  local copies, waits for them, and re-layouts: 5.91 us -> 0 us
    pallas_call x1, Pallas kernels: 126 us -> 100 us  [on_device(): pl.pallas_call(functools.partial(kernel, dp_n, nf), out_shape=(jax.ShapeD...]
    unnamed x12 -> x0, local copies, waits for them, and re-layouts: 5.33 us -> none
    pallas_call x0 -> x1, Pallas kernels: none -> 2.99 us  [on_device(): pl.pallas_call(hand_out, out_shape=(jax.ShapeDtypeStruct((1, T, HP), BF16...]
where the time goes in v2:
time: 104 us
  Pallas kernels  103 us (99%)
    pallas_call x1, Pallas kernels, on_device(): pl.pallas_call(functools.partial(kernel, dp_n, nf), out_shape=(jax.ShapeD...  100 us
    pallas_call x1, Pallas kernels, on_device(): pl.pallas_call(hand_out, out_shape=(jax.ShapeDtypeStruct((1, T, HP), BF16...  2.99 us

profile of v2, /device:TPU:1, one launch (start us, length us, event | category | flops | bytes accessed | tf_op | source)
XLA Modules:
  0.0 103.8 jit_solution(2457293060399878329)
XLA Ops:
  0.6 100.2 %shard_map.137 = (bf16[256,2048]{1,0:T(8,128)(2,1)}, f32[256,128]{1,0:T(8,128)}, f32[256,128]{1,0:T(8,128)}, f32[32,256]{1,0:T(8,128)}, f32[8,128]{1,0:T(8,128)}) custom-call(bf16[256,2048]{1,0:T(8,128)(2,1)} %bitcast.8, bf16[256,128]{1,0:T(8,128)(2,1)} %bitcast.10, bf16[256,128]{1,0:T(8,128)(2,1)} %bitcast.11, f32[32,256]{1,0:T(8,128)} %bitcast.12, ...), custom_call_target="tpu_custom_call" | custom-call | tf_op jit(solution)/shard_map/pallas_call | solution.py:663
  100.8 3.0 %shard_map.138 = (bf16[1,256,2048]{2,1,0:T(8,128)(2,1)}, f32[1,256,128]{2,1,0:T(8,128)}, f32[1,256,128]{2,1,0:T(8,128)}, f32[1,32,256]{2,1,0:T(8,128)}, f32[3,32]{1,0:T(4,128)}) custom-call(bf16[256,2048]{1,0:T(8,128)(2,1)} %get-tuple-element.10.gx, f32[256,128]{1,0:T(8,128)} %get-tuple-element.11.gb, f32[256,128]{1,0:T(8,128)} %get-tuple-element.12.gc, ...), custom_call_target="tpu_custom_call" | custom-call | tf_op jit(solution)/shard_map/pallas_call | solution.py:752

commit v3 on v2

--- a/solution.py
+++ b/solution.py
@@ -228,7 +228,7 @@
     def block(i):
         return pl.ds(pl.multiple_of(i * WB, WB), WB)
 
-    @pl.loop(0, BLOCKS, unroll=2)
+    @pl.loop(0, BLOCKS, unroll=4)
     def _(i):
         blk = block(i)
         e3 = e96[:, blk]
@@ -398,7 +398,7 @@
 
     vel[...] = jnp.zeros_like(vel)
 
-    @pl.loop(0, BLOCKS, unroll=2)
+    @pl.loop(0, BLOCKS, unroll=8)
     def _(i):
         blk = block(i)
         state = s_in[:, blk]
@@ -580,7 +580,7 @@
     gd_all = jnp.where(first, gd_sib[...] + decay_sib * gd_all, gd_all)
     gdh, gdl = split(gd_all[:, 0 : FEET * H])
 
-    @pl.loop(0, BLOCKS, unroll=2)
+    @pl.loop(0, BLOCKS, unroll=4)
     def _(i):
         blk = block(i)
         eh = e96[0:H, blk]
@@ -627,7 +627,7 @@
         ghi, glo = split(g_end[:, blk])
         gb_ref[...] += nt(hi, ghi) + nt(lo, ghi) + nt(hi, glo)
 
-    pl.loop(0, BLOCKS // 2, unroll=2)(sources)
+    pl.loop(0, BLOCKS // 2, unroll=4)(sources)
     arrived(hgot1, G1 - 1, 16)
     hmid[...] = jnp.sum(hgot1[...], axis=0)
 
@@ -637,7 +637,7 @@
         remote(hmid, hgot2.at[spot], 17, 17, frame, dp).start()
 
     hgot2[spot] = hmid[...]
-    pl.loop(BLOCKS // 2, BLOCKS, unroll=2)(sources)
+    pl.loop(BLOCKS // 2, BLOCKS, unroll=4)(sources)
     arrived(hgot2, g2n - 1, 17)
     hg_ref[...] = jnp.sum(hgot2[...], axis=0)
 

time: 104 us -> 103 us (level)
  no operation moved by 1% of the time
where the time goes in v3:
time: 103 us
  Pallas kernels  102 us (99%)
    pallas_call x1, Pallas kernels, on_device(): pl.pallas_call(functools.partial(kernel, dp_n, nf), out_shape=(jax.ShapeD...  99.5 us
    pallas_call x1, Pallas kernels, on_device(): pl.pallas_call(hand_out, out_shape=(jax.ShapeDtypeStruct((1, T, HP), BF16...  2.99 us

profile of v3, /device:TPU:1, one launch (start us, length us, event | category | flops | bytes accessed | tf_op | source)
XLA Modules:
  0.0 103.1 jit_solution(11602275311449237862)
XLA Ops:
  0.6 99.5 %shard_map.137 = (bf16[256,2048]{1,0:T(8,128)(2,1)}, f32[256,128]{1,0:T(8,128)}, f32[256,128]{1,0:T(8,128)}, f32[32,256]{1,0:T(8,128)}, f32[8,128]{1,0:T(8,128)}) custom-call(bf16[256,2048]{1,0:T(8,128)(2,1)} %bitcast.8, bf16[256,128]{1,0:T(8,128)(2,1)} %bitcast.10, bf16[256,128]{1,0:T(8,128)(2,1)} %bitcast.11, f32[32,256]{1,0:T(8,128)} %bitcast.12, ...), custom_call_target="tpu_custom_call" | custom-call | tf_op jit(solution)/shard_map/pallas_call | solution.py:663
  100.1 3.0 %shard_map.138 = (bf16[1,256,2048]{2,1,0:T(8,128)(2,1)}, f32[1,256,128]{2,1,0:T(8,128)}, f32[1,256,128]{2,1,0:T(8,128)}, f32[1,32,256]{2,1,0:T(8,128)}, f32[3,32]{1,0:T(4,128)}) custom-call(bf16[256,2048]{1,0:T(8,128)(2,1)} %get-tuple-element.10.gx, f32[256,128]{1,0:T(8,128)} %get-tuple-element.11.gb, f32[256,128]{1,0:T(8,128)} %get-tuple-element.12.gc, ...), custom_call_target="tpu_custom_call" | custom-call | tf_op jit(solution)/shard_map/pallas_call | solution.py:752
